TPU v7x, 256 devices: a whole 4x4x8 slice. The times are simulated.
256 devices in a mesh: dp: 16 (over x, z_lo, core), ctx: 16 (over y, z_hi).
Axes of the slice: x: 4, y: 4, z: 8 (z_hi: 4, z_lo: 2; z = z_hi * 2 + z_lo), core: 2. Of those that a mesh axis runs over, the one named last changes fastest.
Arguments:
- queries: bfloat16 [16, 4096, 2048], P('dp', 'ctx'), may hold values from -4.5 to 4.5
- keys: bfloat16 [16, 4096, 2048], P('dp', 'ctx'), may hold values from -4.5 to 4.5
- values: bfloat16 [16, 4096, 2048], P('dp', 'ctx'), may hold values from -6 to 6
- out_grad: bfloat16 [16, 4096, 2048], P('dp', 'ctx'), may hold values from -6 to 6
- chosen: int32 [16, 16], P('dp'), may hold values from -1 to 31, as said below
- proj: bfloat16 [2048, 2048], P('ctx', 'dp'), may hold values from -0.125 to 0.125
Outputs:
- attn_out: bfloat16 [16, 4096, 2048], P('dp', 'ctx')
- q_grad: bfloat16 [16, 4096, 2048], P('dp', 'ctx')
- k_grad: bfloat16 [16, 4096, 2048], P('dp', 'ctx')
- v_grad: bfloat16 [16, 4096, 2048], P('dp', 'ctx')
- proj_grad: float32 [2048, 2048], P('ctx', 'dp')
Inputs may be any that keep to these rules, and one draw needn't show every extreme that they name: chosen[d, c] is -1 or the index pos // 128 of one of the blocks that ctx index c stores (position spans c and 31 - c, of 1 block each); every sequence has one or more entries that are not -1.
All inputs are finite; a program needn't handle non-finite values.
Results may differ from a plain program's by a relative error of at most 0.023.
Values may be sent and summed in bfloat16 or wider, within the bound.
No kernel may reach another device: no remote copies, remote signals or barrier semaphores. Data moves between devices by JAX's collectives and lax.ppermute only.
A program may use at most 192 MiB of HBM per device.

v0:
```python
import math

import jax
import jax.numpy as jnp
from jax import lax
from jax.sharding import PartitionSpec as P

BLOCK = 128


def cross_dot(left_op, right_op):
    return lax.dot_general(
        left_op, right_op, (((1,), (1,)), ((), ())), preferred_element_type=jnp.float32
    )


def inner_dot(left_op, right_op):
    return lax.dot_general(
        left_op, right_op, (((0,), (0,)), ((), ())), preferred_element_type=jnp.float32
    )


def head_probs(
    query_block,
    query_pos,
    query_live,
    query_ids,
    heads_k,
    slot_pos,
    slot_live,
    slot_ids,
    score_scale,
):
    scores = cross_dot(query_block, heads_k) * score_scale
    allowed = query_live[:, None] & slot_live[None, :] & (
        slot_pos[None, :] <= query_pos[:, None]
    ) | (query_ids[:, None] == slot_ids[None, :])
    masked = jnp.where(allowed, scores, -1e30)
    row_max = jnp.max(masked, axis=1, keepdims=True)
    exp_terms = jnp.where(allowed, jnp.exp(masked - row_max), 0.0)
    return exp_terms / jnp.sum(exp_terms, axis=1, keepdims=True)


def shards(queries, keys, values, out_grad, chosen, proj):
    ctx_count = lax.axis_size("ctx")
    ctx_index = lax.axis_index("ctx")
    tokens = queries.shape[1]
    half_rows = tokens // 2
    block_rows = BLOCK
    dout = out_grad.shape[2]
    picked = chosen[0]
    own_pick = lax.dynamic_index_in_dim(picked, ctx_index, 0, keepdims=False)
    own_live = own_pick >= 0
    first_pos = jnp.where(own_live, own_pick, 0) * block_rows
    local_row = jnp.where(
        first_pos // half_rows == ctx_index,
        first_pos % half_rows,
        half_rows + first_pos % half_rows,
    )
    row_start = jnp.where(own_live, local_row, 0)

    def take_rows(source):
        slot_block = lax.dynamic_slice_in_dim(source[0], row_start, block_rows, 0)
        return jnp.where(own_live, slot_block, jnp.zeros((), source.dtype))

    def place_rows(slot_block, template):
        return lax.dynamic_update_slice_in_dim(
            jnp.zeros(template.shape, jnp.bfloat16), slot_block[None], row_start, 1
        )

    q_slot = take_rows(queries)
    k_slot = take_rows(keys)
    v_slot = take_rows(values)
    g_slot = take_rows(out_grad)
    heads_q, heads_k, heads_v = (
        lax.all_to_all(q_slot, "ctx", split_axis=1, concat_axis=0, tiled=True),
        lax.all_to_all(k_slot, "ctx", split_axis=1, concat_axis=0, tiled=True),
        lax.all_to_all(v_slot, "ctx", split_axis=1, concat_axis=0, tiled=True),
    )
    slot_count = ctx_count * block_rows
    offsets = jnp.arange(block_rows, dtype=jnp.int32)
    safe_pick = jnp.where(picked >= 0, picked, 0)
    slot_pos = (safe_pick[:, None] * block_rows + offsets[None, :]).reshape(slot_count)
    slot_live = jnp.repeat(picked >= 0, block_rows)
    slot_ids = jnp.arange(slot_count, dtype=jnp.int32)
    head_dim = heads_q.shape[1]
    score_scale = 1.0 / math.sqrt(head_dim)
    step_rows = min(512, slot_count)
    step_count = slot_count // step_rows
    attn_parts = []
    prob_store = []
    prob_b_store = []
    for step_index in range(step_count):
        row_low = step_index * step_rows
        window = slice(row_low, row_low + step_rows)
        attn_prob = head_probs(
            heads_q[window],
            slot_pos[window],
            slot_live[window],
            slot_ids[window],
            heads_k,
            slot_pos,
            slot_live,
            slot_ids,
            score_scale,
        )
        prob_b = attn_prob.astype(jnp.bfloat16)
        prob_store.append(attn_prob)
        prob_b_store.append(prob_b)
        attn_parts.append(
            jnp.dot(prob_b, heads_v, preferred_element_type=jnp.float32).astype(jnp.bfloat16)
        )
    attn_heads = jnp.concatenate(attn_parts, 0)
    attn_local = lax.all_to_all(attn_heads, "ctx", split_axis=0, concat_axis=1, tiled=True)
    head_rows = lax.all_gather(proj, "dp", axis=1, tiled=True)
    full_proj = lax.all_gather(head_rows, "ctx", axis=0, tiled=True)
    mixed = jnp.dot(attn_local, full_proj, preferred_element_type=jnp.float32).astype(jnp.bfloat16)
    attn_out = place_rows(mixed, out_grad)
    attn_grad_local = cross_dot(g_slot, full_proj).astype(jnp.bfloat16)
    dp_count = lax.axis_size("dp")
    weight_term = jnp.einsum(
        "io,inr->nor",
        attn_local,
        g_slot.reshape(block_rows, dp_count, dout // dp_count),
        preferred_element_type=jnp.float32,
    )
    proj_grad = lax.psum_scatter(
        weight_term.reshape(dp_count * full_proj.shape[0], dout // dp_count),
        ("dp", "ctx"),
        scatter_dimension=0,
        tiled=True,
    )
    attn_grad = lax.all_to_all(attn_grad_local, "ctx", split_axis=1, concat_axis=0, tiled=True)
    key_grad = jnp.zeros((slot_count, head_dim), jnp.float32)
    value_grad = jnp.zeros((slot_count, head_dim), jnp.float32)
    query_parts = []
    for step_index in range(step_count):
        row_low = step_index * step_rows
        window = slice(row_low, row_low + step_rows)
        attn_prob = prob_store[step_index]
        prob_b = prob_b_store[step_index]
        grad_block = attn_grad[window]
        row_delta = jnp.sum(
            grad_block.astype(jnp.float32) * attn_heads[window].astype(jnp.float32),
            axis=1,
            keepdims=True,
        )
        score_grad = (attn_prob * (cross_dot(grad_block, heads_v) - row_delta)).astype(jnp.bfloat16)
        query_parts.append(
            (jnp.dot(score_grad, heads_k, preferred_element_type=jnp.float32) * score_scale).astype(
                jnp.bfloat16
            )
        )
        key_grad = key_grad + inner_dot(score_grad, heads_q[window])
        value_grad = value_grad + inner_dot(prob_b, grad_block)
    q_heads_grad = jnp.concatenate(query_parts, 0)
    k_heads_grad = (key_grad * score_scale).astype(jnp.bfloat16)
    v_heads_grad = value_grad.astype(jnp.bfloat16)
    q_back, k_back, v_back = (
        lax.all_to_all(q_heads_grad, "ctx", split_axis=0, concat_axis=1, tiled=True),
        lax.all_to_all(k_heads_grad, "ctx", split_axis=0, concat_axis=1, tiled=True),
        lax.all_to_all(v_heads_grad, "ctx", split_axis=0, concat_axis=1, tiled=True),
    )
    return (
        attn_out,
        place_rows(q_back, queries),
        place_rows(k_back, keys),
        place_rows(v_back, values),
        proj_grad,
    )


def solution(mesh):
    placed = (
        P("dp", "ctx", None),
        P("dp", "ctx", None),
        P("dp", "ctx", None),
        P("dp", "ctx", None),
        P("dp", None),
        P("ctx", "dp"),
    )
    return jax.shard_map(
        shards,
        mesh=mesh,
        in_specs=placed,
        out_specs=(
            P("dp", "ctx", None),
            P("dp", "ctx", None),
            P("dp", "ctx", None),
            P("dp", "ctx", None),
            P("ctx", "dp"),
        ),
        check_vma=False,
    )
```

profile of v0, /device:TPU:0, one launch (start us, length us, event | category | flops | bytes accessed | tf_op | source)
XLA Modules:
  0.0 1589.2 jit_solution(10697018484163687132)
XLA Ops:
  7.2 22.2 %all_gather.6 = bf16[128,2048]{1,0:T(8,128)(2,1)} all-gather(bf16[128,128]{1,0:T(8,128)(2,1)} %param.11), channel_id=1, replica_groups=mesh['dp'=16,'ctx'=16] {'dp'}, dimensions={1}, use_global_device_ids=true | all-gather | bytes 557056 | tf_op jit(solution)/shard_map/all_gather | solution.py:115
  29.4 1.2 constant_dynamic-slice_fusion.4
  32.0 1.5 constant_dynamic-slice_fusion.2
  33.8 0.8 broadcast_select_fusion.2
  34.6 10.3 all-to-all-start.1
  45.0 1.3 constant_dynamic-slice_fusion
  47.1 0.8 broadcast_select_fusion.3
  47.9 26.1 %all-to-all-done.1 = bf16[128,16,128]{0,2,1:T(8,128)(2,1)S(1)} async-done(((bf16[128,16,128]{0,2,1:T(8,128)(2,1)}), bf16[128,16,128]{0,2,1:T(8,128)(2,1)S(1)}, u32[]{:S(2)}, u32[]{:S(2)}) %all-to-all-start.1) | async-done | bytes 524320 | tf_op jit(solution)/shard_map/all_to_all | solution.py:77
  74.0 4.8 all-to-all-start
  79.7 14.8 all-to-all-done
  94.5 3.7 all-to-all-start.2
  99.5 29.0 %all-to-all-done.2 = bf16[128,16,128]{0,2,1:T(8,128)(2,1)S(1)} async-done(((bf16[128,16,128]{0,2,1:T(8,128)(2,1)}), bf16[128,16,128]{0,2,1:T(8,128)(2,1)S(1)}, u32[]{:S(2)}, u32[]{:S(2)}) %all-to-all-start.2) | async-done | bytes 524320 | tf_op jit(solution)/shard_map/all_to_all | solution.py:78
  130.3 1.9 fusion.7
  132.3 7.6 fusion.4
  139.9 7.6 fusion.10
  147.5 7.3 fusion.11
  154.8 14.9 all-gather.2.cloned.1.call-done
  169.7 6.3 fusion.20
  176.0 0.9 copy.51
  176.9 11.4 all-to-all-start.4
  188.3 9.9 fusion.9
  198.2 7.3 all-to-all-done.4
  205.5 3.1 multiply_reduce_fusion.2
  212.5 18.8 %all_to_all.128 = bf16[16,128,128]{2,1,0:T(8,128)(2,1)S(1)} all-to-all(bf16[16,128,128]{2,1,0:T(8,128)(2,1)S(1)} %bitcast.147), channel_id=1, replica_groups=mesh['dp'=16,'ctx'=16] {'ctx'}, dimensions={0} | all-to-all | bytes 1048576 | tf_op jit(solution)/shard_map/all_to_all | solution.py:114
  232.7 8.1 convolution_bitcast_fusion
  240.7 17.6 %copy.39 = f32[16,2048,128]{2,1,0:T(8,128)} copy(f32[16,2048,128]{1,2,0:T(8,128)} %convolution_bitcast_fusion) | data formatting | bytes 33554432 | tf_op jit(solution)/shard_map/io,inr->nor/transpose | solution.py:121
  258.3 3.1 fusion.31
  262.5 1.2 copy-done.7
  265.1 1.6 fusion.18
  266.6 5.3 all-to-all-start.7
  272.0 3.1 multiply_convert_fusion
  283.9 3.9 all-to-all-done.7
  287.8 6.3 all-to-all-start.5
  294.2 2.5 convolution_add_fusion.5
  297.5 1.6 fusion.17
  299.0 11.6 all-to-all-done.5
  310.6 3.9 all-to-all-start.6
  314.5 1.4 copy.38
  316.1 1.4 copy.36
  317.8 12.0 all-to-all-done.6
  330.3 4.6 fusion.19
  335.0 1.1 broadcast.76.clone
  336.1 3.8 dynamic_update_slice.12
  340.0 2.9 dynamic_update_slice.15
  342.9 1.2 broadcast.76.clone.1
  344.2 3.8 dynamic_update_slice.13
  348.2 2.9 dynamic_update_slice.14
  351.1 1231.0 %reduce-scatter.2.cloned.1.call-done = f32[128,128]{1,0:T(8,128)} async-done(((f32[32768,128]{1,0:T(8,128)}), f32[128,128]{1,0:T(8,128)}) %reduce-scatter.2.cloned.1.call-update) | async-done | bytes 65552 | tf_op jit(solution)/shard_map/reduce_scatter | solution.py:127
  (113 shorter events, 23.5 us)
Async XLA Ops:
  7.2 37.8 %copy-start.29 = (s32[1,16]{1,0:T(1,128)S(1)}, s32[1,16]{1,0:T(1,128)}, u32[]{:S(2)}) copy-start(s32[1,16]{1,0:T(1,128)} %param.10) | copy-start | bytes 196
  7.2 37.8 %copy-start.28 = (bf16[1,256,2048]{2,1,0:T(8,128)(2,1)S(1)}, bf16[1,256,2048]{2,1,0:T(8,128)(2,1)}, u32[]{:S(2)}) copy-start(bf16[1,256,2048]{2,1,0:T(8,128)(2,1)} %param.9) | copy-start | bytes 3145732
  7.2 162.5 %all-gather.2.cloned.1.call-start = ((), (), s32[]{:S(2)}) async-start(), calls=%async_computation.9 | async-start | bytes 8912896 | tf_op jit(solution)/shard_map/all_gather | solution.py:116
  34.6 39.3 %all-to-all-start.1 = ((bf16[128,16,128]{0,2,1:T(8,128)(2,1)}), bf16[128,16,128]{0,2,1:T(8,128)(2,1)S(1)}, u32[]{:S(2)}, u32[]{:S(2)}) async-start(bf16[128,16,128]{0,2,1:T(8,128)(2,1)} %bitcast.9), calls=%async_computation.1 | async-start | bytes 1048576 | tf_op jit(solution)/shard_map/all_to_all | solution.py:77
  74.0 20.6 %all-to-all-start = ((bf16[128,16,128]{0,2,1:T(8,128)(2,1)}), bf16[128,16,128]{0,2,1:T(8,128)(2,1)S(1)}, u32[]{:S(2)}, u32[]{:S(2)}) async-start(bf16[128,16,128]{0,2,1:T(8,128)(2,1)} %bitcast.6), calls=%async_computation | async-start | bytes 1048576 | tf_op jit(solution)/shard_map/all_to_all | solution.py:76
  94.5 34.1 %all-to-all-start.2 = ((bf16[128,16,128]{0,2,1:T(8,128)(2,1)}), bf16[128,16,128]{0,2,1:T(8,128)(2,1)S(1)}, u32[]{:S(2)}, u32[]{:S(2)}) async-start(bf16[128,16,128]{0,2,1:T(8,128)(2,1)} %bitcast.12), calls=%async_computation.2 | async-start | bytes 1048576 | tf_op jit(solution)/shard_map/all_to_all | solution.py:78
  99.1 31.2 %copy-start.18 = (bf16[4,128,128]{2,1,0:T(8,128)(2,1)}, bf16[4,128,128]{2,1,0:T(8,128)(2,1)S(1)}, u32[]{:S(2)}) copy-start(bf16[4,128,128]{2,1,0:T(8,128)(2,1)S(1)} %copy.31) | copy-start | bytes 393220
  99.2 31.1 %copy-start.26 = (bf16[4,128,128]{2,1,0:T(8,128)(2,1)}, bf16[4,128,128]{2,1,0:T(8,128)(2,1)S(1)}, u32[]{:S(2)}) copy-start(bf16[4,128,128]{2,1,0:T(8,128)(2,1)S(1)} %copy.32) | copy-start | bytes 393220
  99.4 30.9 %copy-start.20 = (bf16[4,128,128]{2,1,0:T(8,128)(2,1)}, bf16[4,128,128]{2,1,0:T(8,128)(2,1)S(1)}, u32[]{:S(2)}) copy-start(bf16[4,128,128]{2,1,0:T(8,128)(2,1)S(1)} %copy.30) | copy-start | bytes 393220
  99.5 32.7 %copy-start.24 = (bf16[4,128,128]{2,1,0:T(8,128)(2,1)}, bf16[4,128,128]{2,1,0:T(8,128)(2,1)S(1)}, u32[]{:S(2)}) copy-start(bf16[4,128,128]{2,1,0:T(8,128)(2,1)S(1)} %copy.25) | copy-start | bytes 393220
  130.3 9.5 copy-start.9
  139.9 7.6 copy-start.10
  176.9 28.6 %all-to-all-start.4 = ((bf16[128,16,128]{2,0,1:T(8,128)(2,1)}), bf16[128,16,128]{2,0,1:T(8,128)(2,1)S(1)}, u32[]{:S(2)}, u32[]{:S(2)}) async-start(bf16[128,16,128]{2,0,1:T(8,128)(2,1)} %bitcast.121), calls=%async_computation.4 | async-start | bytes 1048576 | tf_op jit(solution)/shard_map/all_to_all | solution.py:133
  188.3 1393.8 %reduce-scatter.2.cloned.1.call-start = ((), (), s32[]{:S(2)}) async-start(), calls=%async_computation.10 | async-start | bytes 16842752 | tf_op jit(solution)/shard_map/reduce_scatter | solution.py:127
  205.5 3.5 copy-start.2
  205.5 52.8 %copy-start.16 = (bf16[4,128,128]{2,1,0:T(8,128)(2,1)}, bf16[4,128,128]{2,1,0:T(8,128)(2,1)S(1)}, u32[]{:S(2)}) copy-start(bf16[4,128,128]{2,1,0:T(8,128)(2,1)S(1)} %get-tuple-element.12) | copy-start | bytes 393220
  205.5 4.7 copy-start.4
  209.0 2.7 copy-start.6
  231.3 0.8 copy-start.14
  258.3 3.5 copy-start
  261.4 2.3 copy-start.7
  262.5 2.5 copy-start.3
  266.6 21.2 %all-to-all-start.7 = ((bf16[16,128,128]{2,1,0:T(8,128)(2,1)}), bf16[16,128,128]{2,1,0:T(8,128)(2,1)}, u32[]{:S(2)}, u32[]{:S(2)}) async-start(bf16[16,128,128]{2,1,0:T(8,128)(2,1)} %bitcast.37), calls=%async_computation.7 | async-start | bytes 1048576 | tf_op jit(solution)/shard_map/all_to_all | solution.py:162
  271.9 3.8 copy-start.8
  275.7 3.0 copy-start.5
  275.8 2.9 copy-start.17
  276.5 1.4 copy-start.11
  276.5 3.5 copy-start.1
  280.8 1.5 copy-start.13
  280.8 2.3 copy-start.25
  282.3 11.9 copy-start.21
  283.8 12.8 copy-start.19
  287.8 22.8 %all-to-all-start.5 = ((bf16[16,128,128]{2,1,0:T(8,128)(2,1)}), bf16[16,128,128]{2,1,0:T(8,128)(2,1)}, u32[]{:S(2)}, u32[]{:S(2)}) async-start(bf16[16,128,128]{2,1,0:T(8,128)(2,1)} %bitcast.145), calls=%async_computation.5 | async-start | bytes 1048576 | tf_op jit(solution)/shard_map/all_to_all | solution.py:160
  294.2 2.5 copy-start.12
  294.2 3.3 copy-start.27
  299.0 31.3 %copy-start.15 = (bf16[16,128,128]{2,1,0:T(8,128)(2,1)S(1)}, bf16[16,128,128]{2,1,0:T(8,128)(2,1)}, u32[]{:S(2)}) copy-start(bf16[16,128,128]{2,1,0:T(8,128)(2,1)} %copy-done.14) | copy-start | bytes 1572868
  310.6 19.2 %all-to-all-start.6 = ((bf16[16,128,128]{2,1,0:T(8,128)(2,1)}), bf16[16,128,128]{2,1,0:T(8,128)(2,1)S(1)}, u32[]{:S(2)}, u32[]{:S(2)}) async-start(bf16[16,128,128]{2,1,0:T(8,128)(2,1)} %bitcast.154), calls=%async_computation.6 | async-start | bytes 1048576 | tf_op jit(solution)/shard_map/all_to_all | solution.py:161
  342.9 1.3 copy-start.23
  351.1 1231.0 %copy-start.22 = (bf16[1,256,2048]{2,1,0:T(8,128)(2,1)}, bf16[1,256,2048]{2,1,0:T(8,128)(2,1)S(1)}, u32[]{:S(2)}) copy-start(bf16[1,256,2048]{2,1,0:T(8,128)(2,1)S(1)} %dynamic_update_slice.14) | copy-start | bytes 3145732
Sparse Core Ops, SparseCore 0:
  29.5 140.1 all-gather.1
  258.4 1323.6 reduce-scatter.1
where the time goes:
time: 1590 us
  waiting for transfers between devices  1350 us (85%)
  matrix products  55.2 us (3%)
  local copies, waits for them, and re-layouts  51.9 us (3%)
  starting transfers between devices  45.9 us (3%)
  blocking collectives  41 us (3%)
  other arithmetic  28.3 us (2%)
  between operations  16.3 us (1%)
    reduce_scatter x1, waiting for transfers between devices, shards(): lax.psum_scatter(weight_term.reshape(dp_count * full_proj.shape[0], dout...  1230 us
  transfers between devices with their start and end apart: 9, of which 9 were waited for; matrix products, arithmetic and copies ran while one was open for 6% of the time, Pallas kernels for 0%

commit v1 on v0

v1 whole, which is shorter than its diff:
```python
import math

import jax
import jax.numpy as jnp
from jax import lax
from jax.experimental import pallas as pl
from jax.experimental.pallas import tpu as pltpu
from jax.sharding import PartitionSpec as P

BLK = 128
Y = 4
Z = 4
NC = Y * Z
Y_GROUPS = [[y * Z + z for y in range(Y)] for z in range(Z)]
Z_GROUPS = [[y * Z + z for z in range(Z)] for y in range(Y)]
PAIR = 2 * BLK
NEG = -1e30
VMEM_BYTES = 48 * 1024 * 1024
F32 = jnp.float32
BF16 = jnp.bfloat16


def dot_nt(a, b):
    return lax.dot_general(a, b, (((1,), (1,)), ((), ())), preferred_element_type=F32)


def dot_nn(a, b):
    return lax.dot_general(a, b, (((1,), (0,)), ((), ())), preferred_element_type=F32)


def params():
    return pltpu.CompilerParams(vmem_limit_bytes=VMEM_BYTES)


def cost(flops, nbytes, trans=0):
    return pl.CostEstimate(flops=flops, bytes_accessed=nbytes, transcendentals=trans)


def take_body(where_ref, q_ref, k_ref, v_ref, g_ref, qkv_ref, gs_ref):
    live = where_ref[1] > 0
    zero = jnp.zeros((), BF16)
    heads = qkv_ref.shape[0]
    for h in range(heads):
        cols = slice(h * BLK, (h + 1) * BLK)
        for part, src in enumerate((q_ref, k_ref, v_ref)):
            qkv_ref[h, part * BLK : (part + 1) * BLK, :] = jnp.where(live, src[0, :, cols], zero)
    gs_ref[...] = jnp.where(live, g_ref[0], zero)


def take_rows(where, queries, keys, values, out_grad):
    feats = queries.shape[2]
    steps = 4
    width = feats // steps
    src = pl.BlockSpec((1, BLK, width), lambda i, w: (0, w[0], i))
    return pl.pallas_call(
        take_body,
        grid_spec=pltpu.PrefetchScalarGridSpec(
            num_scalar_prefetch=1,
            grid=(steps,),
            in_specs=[src] * 4,
            out_specs=[
                pl.BlockSpec((NC // steps, 3 * BLK, BLK), lambda i, w: (i, 0, 0)),
                pl.BlockSpec((BLK, width), lambda i, w: (0, i)),
            ],
        ),
        out_shape=[
            jax.ShapeDtypeStruct((NC, 3 * BLK, BLK), BF16),
            jax.ShapeDtypeStruct((BLK, feats), BF16),
        ],
        compiler_params=params(),
        cost_estimate=cost(0, 8 * BLK * feats * 2),
        name="take_rows",
    )(where, queries, keys, values, out_grad)


def attn_grad_body(g_ref, w_ref, out_ref, wide_ref):
    nd = w_ref.shape[0]
    for d in range(nd):
        for b in range(Z):
            wide_ref[b * BLK : (b + 1) * BLK, d * BLK : (d + 1) * BLK] = w_ref[d, b]
    for b in range(Z):
        for a in range(Y):
            out_ref[b, a] = dot_nt(g_ref[a], wide_ref[b * BLK : (b + 1) * BLK, :]).astype(BF16)


def attn_grad_product(gs_y, proj_rows):
    cols = gs_y.shape[2]
    return pl.pallas_call(
        attn_grad_body,
        out_shape=[
            jax.ShapeDtypeStruct((Z, Y, BLK, BLK), BF16),
            jax.ShapeDtypeStruct((Z * BLK, cols), BF16),
        ],
        compiler_params=params(),
        cost_estimate=cost(2 * 512 * 512 * cols, 3 * 512 * cols * 2),
        name="attn_grad_product",
    )(gs_y, proj_rows)


def sort_blocks(chosen_ref, order_ref):
    count = jnp.int32(0)
    for pos in range(2 * NC):
        c = pos if pos < NC else 2 * NC - 1 - pos
        hit = chosen_ref[c] == pos

        @pl.when(hit)
        def _():
            order_ref[count] = c

        count = count + hit.astype(jnp.int32)
    live = count
    for c in range(NC):
        hit = chosen_ref[c] < 0

        @pl.when(hit)
        def _():
            order_ref[count] = c

        count = count + hit.astype(jnp.int32)
    return live


def causal(s):
    key = lax.broadcasted_iota(jnp.int32, s.shape, 0)
    query = lax.broadcasted_iota(jnp.int32, s.shape, 1)
    return jnp.where(key <= query, s, NEG)


def forward_body(chosen_ref, qkv_ref, attn_ref, lse_ref, q_s, k_s, vt_s, order_ref):
    live = sort_blocks(chosen_ref, order_ref)
    scale2 = math.log2(math.e) / math.sqrt(BLK)
    for r in range(NC):
        c = order_ref[r]
        rows = slice(r * BLK, (r + 1) * BLK)

        @pl.when(r // 2 * 2 < live)
        def _():
            q_s[rows, :] = qkv_ref[c, 0:BLK, :]
            k_s[rows, :] = qkv_ref[c, BLK : 2 * BLK, :]
            vt_s[:, rows] = qkv_ref[c, 2 * BLK : 3 * BLK, :].T

        @pl.when(r >= live)
        def _():
            attn_ref[c % Z, c // Z] = jnp.zeros((BLK, BLK), BF16)

    for p in range(NC // 2):

        @pl.when(2 * p < live)
        def _():
            low = p * PAIR
            q2 = q_s[low : low + PAIR, :]
            diag = causal(dot_nt(k_s[low : low + PAIR, :], q2))
            parts = [(low, diag)]
            top = jnp.max(diag, axis=0, keepdims=True)
            for j in range(p):
                s = dot_nt(k_s[j * PAIR : (j + 1) * PAIR, :], q2)
                top = jnp.maximum(top, jnp.max(s, axis=0, keepdims=True))
                parts.append((j * PAIR, s))
            total = jnp.zeros((1, PAIR), F32)
            out_t = jnp.zeros((BLK, PAIR), F32)
            shift = top * scale2
            for start, s in parts:
                e = jnp.exp2(s * scale2 - shift)
                total = total + jnp.sum(e, axis=0, keepdims=True)
                out_t = out_t + dot_nn(vt_s[:, start : start + PAIR], e.astype(BF16))
            lse_ref[p : p + 1, :] = shift + jnp.log2(total)
            out = (out_t * (1.0 / total)).T.astype(BF16)
            for t in range(2):
                c = order_ref[2 * p + t]

                @pl.when(2 * p + t < live)
                def _():
                    attn_ref[c % Z, c // Z] = out[t * BLK : (t + 1) * BLK, :]


def attn_forward(chosen, qkv):
    slots = NC * BLK
    return pl.pallas_call(
        forward_body,
        in_specs=[
            pl.BlockSpec(memory_space=pltpu.SMEM),
            pl.BlockSpec(memory_space=pltpu.VMEM),
        ],
        out_shape=[
            jax.ShapeDtypeStruct((Z, Y, BLK, BLK), BF16),
            jax.ShapeDtypeStruct((NC // 2, PAIR), F32),
        ],
        scratch_shapes=[
            pltpu.VMEM((slots, BLK), BF16),
            pltpu.VMEM((slots, BLK), BF16),
            pltpu.VMEM((BLK, slots), BF16),
            pltpu.SMEM((NC,), jnp.int32),
        ],
        compiler_params=params(),
        cost_estimate=cost(2 * 2 * slots * slots * BLK, 4 * slots * BLK * 2, slots * slots),
        name="attn_forward",
    )(chosen, qkv)


def backward_body(
    chosen_ref,
    qkv_ref,
    grad_ref,
    attn_ref,
    lse_ref,
    out_ref,
    q_s,
    k_s,
    v_s,
    g_s,
    kt_s,
    dk_s,
    dv_s,
    order_ref,
):
    live = sort_blocks(chosen_ref, order_ref)
    scale = 1.0 / math.sqrt(BLK)
    scale2 = math.log2(math.e) * scale
    for r in range(NC):
        c = order_ref[r]
        rows = slice(r * BLK, (r + 1) * BLK)

        @pl.when(r // 2 * 2 < live)
        def _():
            k_blk = qkv_ref[c, BLK : 2 * BLK, :]
            q_s[rows, :] = qkv_ref[c, 0:BLK, :]
            k_s[rows, :] = k_blk
            kt_s[:, rows] = k_blk.T
            v_s[rows, :] = qkv_ref[c, 2 * BLK : 3 * BLK, :]
            g_s[rows, :] = grad_ref[c % Z, c // Z]

        @pl.when(r >= live)
        def _():
            out_ref[c] = jnp.zeros((3 * BLK, BLK), BF16)

    for p in range(NC // 2):

        @pl.when(2 * p < live)
        def _():
            low = p * PAIR
            q2 = q_s[low : low + PAIR, :]
            g2 = g_s[low : low + PAIR, :]
            deltas = []
            for t in range(2):
                c = order_ref[2 * p + t]
                prod = g2[t * BLK : (t + 1) * BLK, :].astype(F32) * attn_ref[c % Z, c // Z].astype(F32)
                deltas.append(jnp.sum(prod.T, axis=0, keepdims=True))
            delta = jnp.concatenate(deltas, axis=1)
            lse = lse_ref[p : p + 1, :]
            dq_t = jnp.zeros((BLK, PAIR), F32)
            for j in range(p + 1):
                keys = slice(j * PAIR, (j + 1) * PAIR)
                s = dot_nt(k_s[keys, :], q2)
                if j == p:
                    s = causal(s)
                prob = jnp.exp2(s * scale2 - lse)
                dprob = dot_nt(v_s[keys, :], g2)
                ds = (prob * (dprob - delta)).astype(BF16)
                dv = dot_nn(prob.astype(BF16), g2)
                dk = dot_nn(ds, q2)
                if j == p:
                    dv_s[keys, :] = dv
                    dk_s[keys, :] = dk
                else:
                    dv_s[keys, :] += dv
                    dk_s[keys, :] += dk
                dq_t = dq_t + dot_nn(kt_s[:, keys], ds)
            dq = (dq_t * scale).T.astype(BF16)
            for t in range(2):
                c = order_ref[2 * p + t]

                @pl.when(2 * p + t < live)
                def _():
                    out_ref[c, 0:BLK, :] = dq[t * BLK : (t + 1) * BLK, :]

    for r in range(NC):
        c = order_ref[r]
        rows = slice(r * BLK, (r + 1) * BLK)

        @pl.when(r < live)
        def _():
            out_ref[c, BLK : 2 * BLK, :] = (dk_s[rows, :] * scale).astype(BF16)
            out_ref[c, 2 * BLK : 3 * BLK, :] = dv_s[rows, :].astype(BF16)


def attn_backward(chosen, qkv, grad, attn, lse):
    slots = NC * BLK
    return pl.pallas_call(
        backward_body,
        in_specs=[pl.BlockSpec(memory_space=pltpu.SMEM)] + [pl.BlockSpec(memory_space=pltpu.VMEM)] * 4,
        out_shape=jax.ShapeDtypeStruct((NC, 3 * BLK, BLK), BF16),
        scratch_shapes=[
            pltpu.VMEM((slots, BLK), BF16),
            pltpu.VMEM((slots, BLK), BF16),
            pltpu.VMEM((slots, BLK), BF16),
            pltpu.VMEM((slots, BLK), BF16),
            pltpu.VMEM((BLK, slots), BF16),
            pltpu.VMEM((slots, BLK), F32),
            pltpu.VMEM((slots, BLK), F32),
            pltpu.SMEM((NC,), jnp.int32),
        ],
        compiler_params=params(),
        cost_estimate=cost(5 * 2 * slots * slots * BLK, 8 * slots * BLK * 2, slots * slots),
        name="attn_backward",
    )(chosen, qkv, grad, attn, lse)


def proj_body(attn_ref, wide_ref, g_ref, mix_ref, dw_ref, a_s, at_s):
    @pl.when(pl.program_id(0) == 0)
    def _():
        for b in range(Z):
            for a in range(Y):
                blk = attn_ref[b, a]
                a_s[a * BLK : (a + 1) * BLK, b * BLK : (b + 1) * BLK] = blk
                at_s[b * BLK : (b + 1) * BLK, a * BLK : (a + 1) * BLK] = blk.T

    width = wide_ref.shape[1]
    for a in range(Y):
        mix_ref[a] = dot_nn(a_s[a * BLK : (a + 1) * BLK, :], wide_ref[...]).astype(BF16)
    grads = g_ref[...].reshape(Y * BLK, width)
    for b in range(Z):
        part = dot_nn(at_s[b * BLK : (b + 1) * BLK, :], grads).astype(BF16)
        for d in range(width // BLK):
            dw_ref[d, b] = part[:, d * BLK : (d + 1) * BLK]


def proj_products(attn_p, wide, gs_y):
    cols = wide.shape[1]
    steps = 4
    width = cols // steps
    return pl.pallas_call(
        proj_body,
        grid=(steps,),
        in_specs=[
            pl.BlockSpec((Z, Y, BLK, BLK), lambda i: (0, 0, 0, 0)),
            pl.BlockSpec((Z * BLK, width), lambda i: (0, i)),
            pl.BlockSpec((Y, BLK, width), lambda i: (0, 0, i)),
        ],
        out_specs=[
            pl.BlockSpec((Y, BLK, width), lambda i: (0, 0, i)),
            pl.BlockSpec((width // BLK, Z, BLK, BLK), lambda i: (i, 0, 0, 0)),
        ],
        out_shape=[
            jax.ShapeDtypeStruct((Y, BLK, cols), BF16),
            jax.ShapeDtypeStruct((cols // BLK, Z, BLK, BLK), BF16),
        ],
        scratch_shapes=[
            pltpu.VMEM((Y * BLK, Z * BLK), BF16),
            pltpu.VMEM((Z * BLK, Y * BLK), BF16),
        ],
        compiler_params=params(),
        cost_estimate=cost(2 * 2 * 512 * 512 * cols, 4 * 512 * cols * 2),
        name="proj_products",
    )(attn_p, wide, gs_y)


def place_mixed_body(where_ref, part_ref, out_ref):
    mine = pl.program_id(0) == where_ref[0]

    @pl.when(mine)
    def _():
        total = part_ref[0].astype(F32)
        for a in range(1, Y):
            total = total + part_ref[a].astype(F32)
        out_ref[0] = total.astype(BF16)

    @pl.when(jnp.logical_not(mine))
    def _():
        out_ref[...] = jnp.zeros(out_ref.shape, BF16)


def place_mixed(where, parts):
    cols = parts.shape[2]
    steps = 2
    width = cols // steps
    return pl.pallas_call(
        place_mixed_body,
        grid_spec=pltpu.PrefetchScalarGridSpec(
            num_scalar_prefetch=1,
            grid=(2, steps),
            in_specs=[pl.BlockSpec((Y, BLK, width), lambda i, j, w: (0, 0, j))],
            out_specs=pl.BlockSpec((1, BLK, width), lambda i, j, w: (0, i, j)),
        ),
        out_shape=jax.ShapeDtypeStruct((1, 2 * BLK, cols), BF16),
        compiler_params=params(),
        cost_estimate=cost(0, 6 * BLK * cols * 2),
        name="place_mixed",
    )(where, parts)


def place_grads_body(where_ref, back_ref, q_ref, k_ref, v_ref):
    mine = pl.program_id(0) == where_ref[0]
    heads = back_ref.shape[0]

    @pl.when(mine)
    def _():
        for h in range(heads):
            cols = slice(h * BLK, (h + 1) * BLK)
            for part, out in enumerate((q_ref, k_ref, v_ref)):
                out[0, :, cols] = back_ref[h, part * BLK : (part + 1) * BLK, :]

    @pl.when(jnp.logical_not(mine))
    def _():
        for out in (q_ref, k_ref, v_ref):
            out[...] = jnp.zeros(out.shape, BF16)


def place_grads(where, back):
    feats = NC * BLK
    steps = 2
    width = feats // steps
    out = pl.BlockSpec((1, BLK, width), lambda i, j, w: (0, i, j))
    shape = jax.ShapeDtypeStruct((1, 2 * BLK, feats), BF16)
    return pl.pallas_call(
        place_grads_body,
        grid_spec=pltpu.PrefetchScalarGridSpec(
            num_scalar_prefetch=1,
            grid=(2, steps),
            in_specs=[pl.BlockSpec((NC // steps, 3 * BLK, BLK), lambda i, j, w: (j, 0, 0))],
            out_specs=[out] * 3,
        ),
        out_shape=[shape] * 3,
        compiler_params=params(),
        cost_estimate=cost(0, 9 * BLK * feats * 2),
        name="place_grads",
    )(where, back)


def shards(queries, keys, values, out_grad, chosen, proj):
    picked = chosen[0]
    ctx_index = lax.axis_index("ctx")
    own_pick = lax.dynamic_index_in_dim(picked, ctx_index, 0, keepdims=False)
    own_live = own_pick >= 0
    second = own_live & (own_pick != ctx_index)
    where = jnp.stack([second, own_live]).astype(jnp.int32)

    rows_z = lax.all_gather(proj, "ctx", axis=0, axis_index_groups=Z_GROUPS)
    proj_rows = lax.all_gather(rows_z, "dp", axis=0)

    qkv_own, gs = take_rows(where, queries, keys, values, out_grad)
    gs_y = lax.all_gather(gs, "ctx", axis=0, axis_index_groups=Y_GROUPS)
    qkv = lax.all_to_all(qkv_own, "ctx", 0, 0, tiled=True)

    grad_p, wide = attn_grad_product(gs_y, proj_rows)
    grad = lax.all_to_all(grad_p, "ctx", 0, 0, tiled=True, axis_index_groups=Z_GROUPS)

    attn, lse = attn_forward(picked, qkv)
    attn_p = lax.all_to_all(attn, "ctx", 0, 0, tiled=True, axis_index_groups=Z_GROUPS)

    back = attn_backward(picked, qkv, grad, attn, lse)
    back = lax.all_to_all(back, "ctx", 0, 0, tiled=True)

    mix_p, dw_p = proj_products(attn_p, wide, gs_y)
    mix_p = lax.all_to_all(mix_p, "ctx", 0, 0, tiled=True, axis_index_groups=Y_GROUPS)
    dw_p = lax.all_to_all(dw_p, "dp", 0, 0, tiled=True)
    dw = jnp.sum(dw_p.astype(F32), axis=0)
    dw = lax.all_to_all(dw, "ctx", 0, 0, tiled=True, axis_index_groups=Z_GROUPS)
    proj_grad = jnp.sum(dw, axis=0)

    attn_out = place_mixed(where, mix_p)
    q_grad, k_grad, v_grad = place_grads(where, back)
    return attn_out, q_grad, k_grad, v_grad, proj_grad


def solution(mesh):
    rows = P("dp", "ctx", None)
    return jax.shard_map(
        shards,
        mesh=mesh,
        in_specs=(rows, rows, rows, rows, P("dp", None), P("ctx", "dp")),
        out_specs=(rows, rows, rows, rows, P("ctx", "dp")),
        check_vma=False,
    )
```

time: 1590 us -> 270 us (0.17)
  waiting for transfers between devices: 1350 us -> 87.7 us
  matrix products: 55.2 us -> 0 us
  blocking collectives: 41 us -> 90.9 us
  local copies, waits for them, and re-layouts: 51.9 us -> 14.3 us
  Pallas kernels: 0 us -> 33 us
  other arithmetic: 28.3 us -> 3.4 us
  starting transfers between devices: 45.9 us -> 23.5 us
    reduce_scatter x1 -> x0, waiting for transfers between devices: 1230 us -> none  [shards(): lax.psum_scatter(weight_term.reshape(dp_count * full_proj.shape[0], dout...]
    all_to_all x1 -> x2, blocking collectives: 18.8 us -> 74.5 us  [the longest x1 43.7 us: shards(): qkv = lax.all_to_all(qkv_own, 'ctx', 0, 0, tiled=True)]
    dot_general x27 -> x0, matrix products: 55.2 us -> none  [the longest x9 22.5 us: cross_dot(): lax.dot_general(left_op, right_op, (((1,), (1,)), ((), ())), preferred_el...]
    all_to_all x7 -> x5, waiting for transfers between devices: 105 us -> 66.7 us  [the longest x1 38.9 us: shards(): back = lax.all_to_all(back, 'ctx', 0, 0, tiled=True)]
    pallas_call x0 -> x7, Pallas kernels: none -> 33 us  [the longest x1 7.09 us: attn_backward(): pl.pallas_call(backward_body, in_specs=[pl.BlockSpec(memory_space=pltpu.S...]
    all_to_all x7 -> x5, starting transfers between devices: 45.8 us -> 23.4 us  [the longest x1 5.7 us: shards(): back = lax.all_to_all(back, 'ctx', 0, 0, tiled=True)]
    transpose x1 -> x0, local copies, waits for them, and re-layouts: 17.6 us -> none  [shards(): jnp.einsum('io,inr->nor', attn_local, g_slot.reshape(block_rows, dp_count...]
    div x2 -> x0, other arithmetic: 17.2 us -> none  [head_probs(): return exp_terms / jnp.sum(exp_terms, axis=1, keepdims=True)]
  transfers between devices with their start and end apart: 9 -> 7, of which waited for: 9 -> 5; matrix products, arithmetic and copies ran while one was open for 6% -> 1% of each run, Pallas kernels for 0% -> 11%
where the time goes in v1:
time: 270 us; the launch traced here: 268 us
  blocking collectives  90.9 us (34%)
  waiting for transfers between devices  87.7 us (32%)
  Pallas kernels  33 us (12%)
  starting transfers between devices  23.5 us (9%)
  between operations  15.4 us (6%)
  local copies, waits for them, and re-layouts  14.3 us (5%)
  other arithmetic  3.4 us (1%)
    all_to_all x1, blocking collectives, shards(): qkv = lax.all_to_all(qkv_own, 'ctx', 0, 0, tiled=True)  43.7 us
    all_to_all x1, waiting for transfers between devices, shards(): back = lax.all_to_all(back, 'ctx', 0, 0, tiled=True)  38.9 us
    all_to_all x1, blocking collectives, shards(): lax.all_to_all(mix_p, 'ctx', 0, 0, tiled=True, axis_index_groups=Y_GROUPS)  30.8 us
    all_gather x1, waiting for transfers between devices, shards(): proj_rows = lax.all_gather(rows_z, 'dp', axis=0)  20.9 us
    all_to_all x1, waiting for transfers between devices, shards(): dw_p = lax.all_to_all(dw_p, 'dp', 0, 0, tiled=True)  18.2 us
    all_gather x1, blocking collectives, shards(): rows_z = lax.all_gather(proj, 'ctx', axis=0, axis_index_groups=Z_GROUPS)  16.4 us
    unnamed x26, local copies, waits for them, and re-layouts  13 us
    all_to_all x1, waiting for transfers between devices, shards(): lax.all_to_all(grad_p, 'ctx', 0, 0, tiled=True, axis_index_groups=Z_GROUPS)  7.74 us
  transfers between devices with their start and end apart: 7, of which 5 were waited for; matrix products, arithmetic and copies ran while one was open for 1% of the time, Pallas kernels for 11%

profile of v1, /device:TPU:0, one launch (start us, length us, event | category | flops | bytes accessed | tf_op | source)
XLA Modules:
  0.0 268.1 jit_solution(2845150846380702991)
XLA Ops:
  7.2 0.0 all-gather.6.cloned.1.call-start
  7.2 1.2 constant_dynamic-slice_fusion
  9.8 0.1 add_convert_fusion.where_ref
  9.8 0.0 copy-start.6
  9.8 1.2 copy-done.6
  11.1 0.0 copy-start.7
  11.1 1.2 copy-done.7
  12.3 0.0 copy-start.8
  12.3 1.2 copy-done.8
  13.5 1.2 copy-done.9
  14.7 2.7 %take_rows.1 = (bf16[16,384,128]{2,1,0:T(8,128)(2,1)}, bf16[128,2048]{1,0:T(8,128)(2,1)}) custom-call(s32[2]{0:T(128)S(1)} %add_convert_fusion.where_ref, bf16[1,256,2048]{2,1,0:T(8,128)(2,1)S(1)} %copy-done.6, bf16[1,256,2048]{2,1,0:T(8,128)(2,1)S(1)} %copy-done.7, bf16[1,256,2048]{2,1,0:T(8,128)(2,1)S(1)} %copy-done.8, bf16[1,256,2048]{2,1,0:T(8,128)(2,1)S(1)} %copy-done.9), custom_call_target="tpu_custom_call" | custom-call | bytes 4194304 | tf_op jit(solution)/shard_map/take_rows/pallas_call | solution.py:55
  17.4 0.0 all-gather.6.cloned.1.call-update
  17.5 0.0 all-gather.8.cloned.1.call-start
  17.5 0.0 copy-done.12
  17.5 16.4 %all-gather.1 = bf16[512,128]{1,0:T(8,128)(2,1)} all-gather(bf16[128,128]{1,0:T(8,128)(2,1)S(1)} %copy-done.12), channel_id=3, replica_groups={{0,1,2,3},{4,5,6,7},{8,9,10,11},{12,13,14,15},{16,17,18,19},{20,21,22,2..., dimensions={0}, use_global_device_ids=true | all-gather | bytes 163840 | tf_op jit(solution)/shard_map/all_gather | solution.py:437
  33.9 0.0 all-gather.8.cloned.1.call-update
  34.0 43.7 %all_to_all.35.qkv_ref = bf16[16,384,128]{2,1,0:T(8,128)(2,1)S(1)} all-to-all(bf16[16,384,128]{2,1,0:T(8,128)(2,1)} %get-tuple-element.16), channel_id=1, replica_groups=mesh['dp'=16,'ctx'=16] {'ctx'}, dimensions={0} | all-to-all | bytes 3145728 | tf_op jit(solution)/shard_map/all_to_all | solution.py:442
  77.7 0.0 copy-done.11
  77.7 6.0 %attn_forward.1 = (bf16[4,4,128,128]{3,2,1,0:T(8,128)(2,1)}, f32[8,256]{1,0:T(8,128)S(1)}) custom-call(s32[16]{0:T(128)S(1)} %bitcast.9, bf16[16,384,128]{2,1,0:T(8,128)(2,1)S(1)} %all_to_all.35.qkv_ref), custom_call_target="tpu_custom_call" | custom-call | flops 2147483648 | bytes 2097152 | tf_op jit(solution)/shard_map/attn_forward/pallas_call | solution.py:178
  83.7 0.0 copy-done.3
  83.7 4.2 %all-to-all-start.1 = ((bf16[4,4,128,128]{3,2,1,0:T(8,128)(2,1)}), bf16[4,4,128,128]{3,2,1,0:T(8,128)(2,1)S(1)}, u32[]{:S(2)}, u32[]{:S(2)}) async-start(bf16[4,4,128,128]{3,2,1,0:T(8,128)(2,1)} %get-tuple-element.17.attn_ref), calls=%async_computation.1 | async-start | bytes 1048576 | tf_op jit(solution)/shard_map/all_to_all | solution.py:448
  87.8 20.9 %all-gather.8.cloned.1.call-done = bf16[64,128,128]{2,1,0:T(8,128)(2,1)} async-done(((bf16[4,128,128]{2,1,0:T(8,128)(2,1)}), bf16[64,128,128]{2,1,0:T(8,128)(2,1)}) %all-gather.8.cloned.1.call-update) | async-done | bytes 2097168 | tf_op jit(solution)/shard_map/all_gather | solution.py:438
  108.8 1.6 copy-done
  110.4 4.7 %attn_grad_product.1 = (bf16[4,4,128,128]{3,2,1,0:T(8,128)(2,1)}, bf16[512,2048]{1,0:T(8,128)(2,1)S(1)}) custom-call(bf16[4,128,2048]{2,1,0:T(8,128)(2,1)S(1)} %bitcast.8, bf16[16,4,128,128]{3,2,1,0:T(8,128)(2,1)} %bitcast.11), custom_call_target="tpu_custom_call" | custom-call | flops 1073741824 | bytes 6291456 | tf_op jit(solution)/shard_map/attn_grad_product/pallas_call | solution.py:88
  115.1 1.3 copy-done.10
  116.4 0.0 all-to-all-done.1.attn_ref
  116.4 5.6 %all-to-all-start.3 = ((bf16[4,4,128,128]{3,2,1,0:T(8,128)(2,1)}), bf16[4,4,128,128]{3,2,1,0:T(8,128)(2,1)S(1)}, u32[]{:S(2)}, u32[]{:S(2)}) async-start(bf16[4,4,128,128]{3,2,1,0:T(8,128)(2,1)} %get-tuple-element.21), calls=%async_computation.3 | async-start | bytes 1048576 | tf_op jit(solution)/shard_map/all_to_all | solution.py:445
  122.0 5.0 %proj_products.1 = (bf16[4,128,2048]{2,1,0:T(8,128)(2,1)S(1)}, bf16[16,4,128,128]{3,2,1,0:T(8,128)(2,1)S(1)}) custom-call(bf16[4,4,128,128]{3,2,1,0:T(8,128)(2,1)S(1)} %all-to-all-done.1.attn_ref, bf16[512,2048]{1,0:T(8,128)(2,1)} %copy-done.10, bf16[4,128,2048]{2,1,0:T(8,128)(2,1)} %bitcast.7), custom_call_target="tpu_custom_call" | custom-call | flops 2147483648 | bytes 8388608 | tf_op jit(solution)/shard_map/proj_products/pallas_call | solution.py:331
  127.1 0.0 copy-start.1
  127.1 1.3 copy-done.1
  128.4 1.3 copy-done.2
  129.7 7.7 %all-to-all-done.3.grad_ref = bf16[4,4,128,128]{3,2,1,0:T(8,128)(2,1)S(1)} async-done(((bf16[4,4,128,128]{3,2,1,0:T(8,128)(2,1)}), bf16[4,4,128,128]{3,2,1,0:T(8,128)(2,1)S(1)}, u32[]{:S(2)}, u32[]{:S(2)}) %all-to-all-start.3) | async-done | bytes 524320 | tf_op jit(solution)/shard_map/all_to_all | solution.py:445
  137.5 30.8 %all_to_all.36.part_ref = bf16[4,128,2048]{2,1,0:T(8,128)(2,1)S(1)} all-to-all(bf16[4,128,2048]{2,1,0:T(8,128)(2,1)} %copy-done.2), channel_id=1, replica_groups={{0,4,8,12},{1,5,9,13},{2,6,10,14},{3,7,11,15},{16,20,24,28},{17,21,25,2..., dimensions={0} | all-to-all | bytes 4194304 | tf_op jit(solution)/shard_map/all_to_all | solution.py:454
  168.3 4.5 %all-to-all-start.5 = ((bf16[16,4,128,128]{3,2,1,0:T(8,128)(2,1)}), bf16[16,4,128,128]{3,2,1,0:T(8,128)(2,1)}, u32[]{:S(2)}, u32[]{:S(2)}) async-start(bf16[16,4,128,128]{3,2,1,0:T(8,128)(2,1)} %copy-done.1), calls=%async_computation.5 | async-start | bytes 4194304 | tf_op jit(solution)/shard_map/all_to_all | solution.py:455
  172.8 0.0 copy-start.4
  172.8 1.4 copy-done.4
  174.2 7.1 %attn_backward.1 = bf16[16,384,128]{2,1,0:T(8,128)(2,1)S(1)} custom-call(s32[16]{0:T(128)S(1)} %bitcast.10, bf16[16,384,128]{2,1,0:T(8,128)(2,1)S(1)} %copy-done.4, bf16[4,4,128,128]{3,2,1,0:T(8,128)(2,1)S(1)} %all-to-all-done.3.grad_ref, bf16[4,4,128,128]{3,2,1,0:T(8,128)(2,1)} %get-tuple-element.17.attn_ref, f32[8,256]{1,0:T(8,128)S(1)} %get-tuple-element.22.lse_ref), custom_call_target="tpu_custom_call" | custom-call | flops 5368709120 | bytes 4194304 | tf_op jit(solution)/shard_map/attn_backward/pallas_call | solution.py:288
  181.3 0.0 copy-start.5
  181.3 1.2 copy-done.5
  182.5 18.2 %all-to-all-done.5 = bf16[16,4,128,128]{3,2,1,0:T(8,128)(2,1)} async-done(((bf16[16,4,128,128]{3,2,1,0:T(8,128)(2,1)}), bf16[16,4,128,128]{3,2,1,0:T(8,128)(2,1)}, u32[]{:S(2)}, u32[]{:S(2)}) %all-to-all-start.5) | async-done | bytes 2097184 | tf_op jit(solution)/shard_map/all_to_all | solution.py:455
  200.7 5.7 %all-to-all-start.4 = ((bf16[16,384,128]{2,1,0:T(8,128)(2,1)}), bf16[16,384,128]{2,1,0:T(8,128)(2,1)}, u32[]{:S(2)}, u32[]{:S(2)}) async-start(bf16[16,384,128]{2,1,0:T(8,128)(2,1)} %copy-done.5), calls=%async_computation.4 | async-start | bytes 3145728 | tf_op jit(solution)/shard_map/all_to_all | solution.py:451
  206.4 2.7 convert_reduce_fusion
  209.1 38.9 %all-to-all-done.4.back_ref = bf16[16,384,128]{2,1,0:T(8,128)(2,1)} async-done(((bf16[16,384,128]{2,1,0:T(8,128)(2,1)}), bf16[16,384,128]{2,1,0:T(8,128)(2,1)}, u32[]{:S(2)}, u32[]{:S(2)}) %all-to-all-start.4) | async-done | bytes 1572896 | tf_op jit(solution)/shard_map/all_to_all | solution.py:451
  247.9 3.4 %all-to-all-start.6 = ((f32[4,128,128]{2,1,0:T(8,128)}), f32[4,128,128]{2,1,0:T(8,128)S(1)}, u32[]{:S(2)}, u32[]{:S(2)}) async-start(f32[4,128,128]{2,1,0:T(8,128)} %convert_reduce_fusion), calls=%async_computation.6 | async-start | bytes 524288 | tf_op jit(solution)/shard_map/all_to_all | solution.py:457
  251.4 2.5 place_mixed.1
  253.9 4.9 %place_grads.1 = (bf16[1,256,2048]{2,1,0:T(8,128)(2,1)}, bf16[1,256,2048]{2,1,0:T(8,128)(2,1)}, bf16[1,256,2048]{2,1,0:T(8,128)(2,1)}) custom-call(s32[2]{0:T(128)S(1)} %add_convert_fusion.where_ref, bf16[16,384,128]{2,1,0:T(8,128)(2,1)} %all-to-all-done.4.back_ref), custom_call_target="tpu_custom_call" | custom-call | bytes 4718592 | tf_op jit(solution)/shard_map/place_grads/pallas_call | solution.py:414
  258.8 1.9 all-to-all-done.6
  260.7 0.6 reduce_sum.19
  (8 shorter events, 0.0 us)
Async XLA Ops:
  7.2 80.7 %all-gather.6.cloned.1.call-start = ((), (), s32[]{:S(2)}) async-start(), calls=%async_computation.7 | async-start | bytes 2621440 | tf_op jit(solution)/shard_map/all_gather | solution.py:441
  9.8 1.2 copy-start.6
  11.1 1.2 copy-start.7
  12.3 1.2 copy-start.8
  13.5 1.2 copy-start.9
  14.7 2.8 %copy-start.12 = (bf16[128,128]{1,0:T(8,128)(2,1)S(1)}, bf16[128,128]{1,0:T(8,128)(2,1)}, u32[]{:S(2)}) copy-start(bf16[128,128]{1,0:T(8,128)(2,1)} %param.11) | copy-start | bytes 98308
  17.4 60.2 %copy-start.11 = (s32[1,16]{1,0:T(1,128)S(1)}, s32[1,16]{1,0:T(1,128)}, u32[]{:S(2)}) copy-start(s32[1,16]{1,0:T(1,128)} %param.10) | copy-start | bytes 196
  17.5 91.3 %all-gather.8.cloned.1.call-start = ((), (), s32[]{:S(2)}) async-start(), calls=%async_computation.8 | async-start | bytes 2228224 | tf_op jit(solution)/shard_map/all_gather | solution.py:438
  77.7 6.0 %copy-start.3 = (bf16[16,384,128]{2,1,0:T(8,128)(2,1)}, bf16[16,384,128]{2,1,0:T(8,128)(2,1)S(1)}, u32[]{:S(2)}) copy-start(bf16[16,384,128]{2,1,0:T(8,128)(2,1)S(1)} %all_to_all.35.qkv_ref) | copy-start | bytes 4718596
  83.7 32.7 %all-to-all-start.1 = ((bf16[4,4,128,128]{3,2,1,0:T(8,128)(2,1)}), bf16[4,4,128,128]{3,2,1,0:T(8,128)(2,1)S(1)}, u32[]{:S(2)}, u32[]{:S(2)}) async-start(bf16[4,4,128,128]{3,2,1,0:T(8,128)(2,1)} %get-tuple-element.17.attn_ref), calls=%async_computation.1 | async-start | bytes 1048576 | tf_op jit(solution)/shard_map/all_to_all | solution.py:448
  108.8 1.6 copy-start
  115.1 1.3 copy-start.10
  116.4 21.1 %all-to-all-start.3 = ((bf16[4,4,128,128]{3,2,1,0:T(8,128)(2,1)}), bf16[4,4,128,128]{3,2,1,0:T(8,128)(2,1)S(1)}, u32[]{:S(2)}, u32[]{:S(2)}) async-start(bf16[4,4,128,128]{3,2,1,0:T(8,128)(2,1)} %get-tuple-element.21), calls=%async_computation.3 | async-start | bytes 1048576 | tf_op jit(solution)/shard_map/all_to_all | solution.py:445
  127.1 1.3 copy-start.1
  128.4 1.3 copy-start.2
  168.3 32.4 %all-to-all-start.5 = ((bf16[16,4,128,128]{3,2,1,0:T(8,128)(2,1)}), bf16[16,4,128,128]{3,2,1,0:T(8,128)(2,1)}, u32[]{:S(2)}, u32[]{:S(2)}) async-start(bf16[16,4,128,128]{3,2,1,0:T(8,128)(2,1)} %copy-done.1), calls=%async_computation.5 | async-start | bytes 4194304 | tf_op jit(solution)/shard_map/all_to_all | solution.py:455
  172.8 1.4 copy-start.4
  181.3 1.2 copy-start.5
  200.7 47.3 %all-to-all-start.4 = ((bf16[16,384,128]{2,1,0:T(8,128)(2,1)}), bf16[16,384,128]{2,1,0:T(8,128)(2,1)}, u32[]{:S(2)}, u32[]{:S(2)}) async-start(bf16[16,384,128]{2,1,0:T(8,128)(2,1)} %copy-done.5), calls=%async_computation.4 | async-start | bytes 3145728 | tf_op jit(solution)/shard_map/all_to_all | solution.py:451
  247.9 12.7 %all-to-all-start.6 = ((f32[4,128,128]{2,1,0:T(8,128)}), f32[4,128,128]{2,1,0:T(8,128)S(1)}, u32[]{:S(2)}, u32[]{:S(2)}) async-start(f32[4,128,128]{2,1,0:T(8,128)} %convert_reduce_fusion), calls=%async_computation.6 | async-start | bytes 524288 | tf_op jit(solution)/shard_map/all_to_all | solution.py:457
Sparse Core Ops, SparseCore 0:
  17.6 45.6 all-gather.5
  65.1 43.6 all-gather.7
